TPU v7x, 32 devices: a whole 2x2x4 slice. The times are simulated.
32 devices in a mesh: groups: 2 (over x), pair: 8 (over z, y), lam: 2 (over core).
Axes of the slice: x: 2, y: 2, z: 4, core: 2. Of those that a mesh axis runs over, the one named last changes fastest.
Arguments:
- integrals: bfloat16 [160, 1024, 1024], P(('groups', 'pair'), 'lam'), parts along dimension 0, may hold values from -6 to 6
- occ_coef: bfloat16 [1024, 32], replicated, may hold values from -0.1875 to 0.1875
- virt_coef: bfloat16 [1024, 974], replicated, may hold values from -0.1875 to 0.1875
- pair_nu: int32 [160], P('groups'), parts along dimension 0, may hold values from 0 to 1023, as said below
Outputs:
- transformed: float32 [4, 32, 32, 974], P('groups', None, 'pair', 'lam'), parts along dimension 0
There are 2 independent parts, one for each index of `groups`. A program takes and returns all parts, laid end to end along the dimension named above; an argument that names none is the same for every part. Nothing has to cross between parts.
Inputs may be any that keep to these rules, and one draw needn't show every extreme that they name: `pair_nu`: within each block of 40 consecutive pairs the numbers are distinct, and every block holds 0 and 1023.
All inputs are finite; a program needn't handle non-finite values.
Results may differ from a plain program's by a relative error of at most 0.0029.
Values may be sent and summed in bfloat16 or wider, within the bound.
A program may use at most 64 MiB of HBM per device.

v0:
```python
import jax
import jax.numpy as jnp
from jax import lax
from jax.sharding import PartitionSpec as P

MUS = 2


def contract_last(mo_block, occ_coef, order_ids, mu_ids):
    count = mo_block.shape[0]
    rows = occ_coef[order_ids].astype(jnp.float32)
    onehot = (mu_ids[:, None] == jnp.arange(MUS, dtype=jnp.int32)[None, :]).astype(jnp.float32)
    weights = (onehot[:, :, None] * rows[:, None, :]).reshape(count, MUS * rows.shape[1])
    flat = mo_block.reshape(count, -1)
    result = lax.dot_general(
        weights, flat, (((0,), (0,)), ((), ())), precision=lax.Precision.HIGHEST
    )
    return result.reshape(MUS, rows.shape[1], mo_block.shape[1], mo_block.shape[2])


def shards(integrals, occ_coef, virt_coef, pair_nu):
    local_pairs = integrals.shape[0]
    half_rows = integrals.shape[1]
    lam_index = lax.axis_index("lam")
    occ_rows = lax.dynamic_slice_in_dim(occ_coef, lam_index * half_rows, half_rows, 0)
    partial_value = jnp.einsum(
        "li,pls->pis", occ_rows, integrals, preferred_element_type=jnp.float32
    )
    pairs_all = pair_nu.shape[0]
    width = pairs_all // MUS
    pair_count = lax.axis_size("pair")
    lam_count = lax.axis_size("lam")
    summed = lax.psum_scatter(partial_value, "lam", scatter_dimension=0, tiled=True)
    half_done = summed.astype(jnp.bfloat16)
    mo_pairs = jnp.einsum("pis,sa->pia", half_done, virt_coef, preferred_element_type=jnp.float32)
    moved = lax.all_to_all(
        lax.all_to_all(mo_pairs, "pair", split_axis=1, concat_axis=0, tiled=True),
        "lam",
        split_axis=2,
        concat_axis=0,
        tiled=True,
    )
    order = jnp.arange(pairs_all, dtype=jnp.int32).reshape(
        pair_count, lam_count, local_pairs // lam_count
    )
    order = jnp.transpose(order, (1, 0, 2)).reshape(-1)
    return contract_last(moved, occ_coef, pair_nu[order], order // width)


def solution(mesh):
    in_specs = (P(("groups", "pair"), "lam", None), P(), P(), P("groups"))
    out_specs = P("groups", None, "pair", "lam")
    return jax.shard_map(shards, mesh=mesh, in_specs=in_specs, out_specs=out_specs, check_vma=False)
```

profile of v0, /device:TPU:0, one launch (start us, length us, event | category | flops | bytes accessed | tf_op | source)
XLA Modules:
  0.0 91.5 jit_solution(7907209301435762418)
XLA Ops:
  6.5 0.0 copy-start
  6.5 0.0 reduce-scatter.2.cloned.1.call-start
  6.5 7.1 %convolution_bitcast_fusion = f32[10,32,1024]{2,1,0:T(8,128)} fusion(bf16[10,512,1024]{2,1,0:T(8,128)(2,1)} %param.4, bf16[1024,32]{0,1:T(8,128)(2,1)} %param.5, s32[]{:T(128)S(6)} %select_n.35), kind=kOutput, calls=%fused_computation.4 | convolution fusion | flops 335544320 | bytes 11829252 | tf_op jit(solution)/shard_map/li,pls->pis/dot_general | solution.py:26
  13.7 0.0 reduce-scatter.2.cloned.1.call-update
  13.7 0.0 copy-done.2
  13.7 0.2 copy.30
  13.9 0.1 reshape.157
  14.0 11.3 %reduce-scatter.2.cloned.1.call-done = f32[5,32,1024]{2,1,0:T(8,128)} async-done(((f32[10,32,1024]{2,1,0:T(8,128)}), f32[5,32,1024]{2,1,0:T(8,128)}) %reduce-scatter.2.cloned.1.call-update) | async-done | bytes 655376 | tf_op jit(solution)/shard_map/reduce_scatter | solution.py:33
  25.3 0.0 copy-done
  25.3 1.9 %fusion = f32[5,32,974]{2,1,0:T(8,128)S(1)} fusion(bf16[1024,974]{0,1:T(8,128)(2,1)S(1)} %copy-done, f32[5,32,1024]{2,1,0:T(8,128)} %reduce-scatter.2.cloned.1.call-done), kind=kOutput, calls=%fused_computation.2 | convolution fusion | flops 319324160 | bytes 3273472 | tf_op jit(solution)/shard_map/pis,sa->pia/dot_general | solution.py:35
  27.2 0.0 copy-start.1
  27.2 1.4 %copy.32 = f32[5,32,974]{2,0,1:T(8,128)} copy(f32[5,32,974]{2,1,0:T(8,128)S(1)} %fusion) | data formatting | bytes 1246720 | tf_op jit(solution)/shard_map/pis,sa->pia/dot_general | solution.py:35
  28.6 5.8 %all-to-all-start = ((f32[5,32,974]{2,0,1:T(8,128)}), f32[5,32,974]{2,0,1:T(8,128)S(1)}, u32[]{:S(2)}, u32[]{:S(2)}) async-start(f32[5,32,974]{2,0,1:T(8,128)} %copy.32), calls=%async_computation.1 | async-start | bytes 2097152 | tf_op jit(solution)/shard_map/all_to_all | solution.py:37
  34.4 0.0 copy-done.1
  34.4 1.2 %gather_fusion = s32[80]{0:T(128)S(1)} fusion(s32[80]{0:T(128)S(1)} %copy-done.1, s32[1024]{0:T(1024)S(1)} %pad_clamp_fusion.1), kind=kCustom, calls=%fused_computation | custom fusion | bytes 960 | tf_op jit(solution)/shard_map/gather | solution.py:47
  35.7 0.7 gather_fusion.1
  36.3 0.1 copy.31
  36.4 0.1 div.14
  36.5 0.1 reshape.163
  36.7 23.9 %all-to-all-done = f32[5,32,974]{2,0,1:T(8,128)S(1)} async-done(((f32[5,32,974]{2,0,1:T(8,128)}), f32[5,32,974]{2,0,1:T(8,128)S(1)}, u32[]{:S(2)}, u32[]{:S(2)}) %all-to-all-start) | async-done | bytes 623392 | tf_op jit(solution)/shard_map/all_to_all | solution.py:37
  60.6 1.3 %copy.33 = f32[5,8,4,974]{3,2,0,1:T(4,128)} copy(f32[5,8,4,974]{3,0,2,1:T(8,128)S(1)} %bitcast.42) | data formatting | bytes 1246720 | tf_op jit(solution)/shard_map/all_to_all | solution.py:37
  61.8 2.7 %copy.34 = f32[40,4,974]{0,1,2:T(4,128)} copy(f32[40,4,974]{2,1,0:T(4,128)} %bitcast.44) | data formatting | bytes 1246720 | tf_op jit(solution)/shard_map/all_to_all | solution.py:37
  64.5 4.1 %reshape.210 = f32[2,1,77920]{2,1,0:T(1,128)S(1)} reshape(f32[974,4,40]{2,1,0:T(4,128)} %bitcast.40) | data formatting | bytes 1246720
  68.6 4.2 %all_to_all.33 = f32[2,1,77920]{2,1,0:T(1,128)S(1)} all-to-all(f32[2,1,77920]{2,1,0:T(1,128)S(1)} %reshape.210), channel_id=1, replica_groups=mesh['groups'=2,'pair'=8,'lam'=2] {'lam'}, dimensions={0} | all-to-all | bytes 1246720 | tf_op jit(solution)/shard_map/all_to_all | solution.py:36
  72.8 0.5 broadcast.122
  73.3 2.6 %reduce = f32[2,77920]{1,0:T(2,128)S(1)} reduce(f32[2,1,77920]{2,1,0:T(1,128)S(1)} %all_to_all.33, f32[]{:T(128)} %broadcast.122), dimensions={1}, to_apply=%all_to_all.28.reduce_sub_computation | reduce | bytes 1246724 | tf_op jit(solution)/shard_map/all_to_all | solution.py:36
  76.0 3.4 %reshape.211 = f32[974,4,40]{2,1,0:T(4,128)} reshape(f32[2,77920]{1,0:T(2,128)S(1)} %reduce) | data formatting | bytes 1246720
  79.4 1.9 %copy.35 = f32[40,4,2,487]{3,1,0,2:T(4,128)S(1)} copy(f32[40,4,2,487]{0,1,3,2:T(4,128)} %bitcast.41) | data formatting | bytes 1246720 | tf_op jit(solution)/shard_map/all_to_all | solution.py:36
  81.3 0.7 reshape.158
  82.0 0.7 dot_general.22
  82.7 0.8 fusion.2
  83.5 1.1 %copy.37 = f32[2,32,4,487]{3,2,1,0:T(4,128)} copy(f32[2,32,4,487]{3,1,2,0:T(8,128)S(1)} %fusion.2) | data formatting | bytes 997376 | tf_op jit(solution)/shard_map/dot_general | solution.py:15
  (11 shorter events, 0.1 us)
Async XLA Ops:
  6.5 18.8 %copy-start = (bf16[1024,974]{0,1:T(8,128)(2,1)S(1)}, bf16[1024,974]{0,1:T(8,128)(2,1)}, u32[]{:S(2)}) copy-start(bf16[1024,974]{0,1:T(8,128)(2,1)} %param.6) | copy-start | bytes 5984260
  6.5 18.8 %reduce-scatter.2.cloned.1.call-start = ((), (), s32[]{:S(2)}) async-start(), calls=%async_computation.3 | async-start | bytes 1966080 | tf_op jit(solution)/shard_map/reduce_scatter | solution.py:33
  6.5 7.2 %copy-start.2 = (bf16[1024,32]{0,1:T(8,128)(2,1)S(1)}, bf16[1024,32]{0,1:T(8,128)(2,1)}, u32[]{:S(2)}) copy-start(bf16[1024,32]{0,1:T(8,128)(2,1)} %param.5) | copy-start | bytes 196612
  27.2 7.2 %copy-start.1 = (s32[80]{0:T(128)S(1)}, s32[80]{0:T(128)}, u32[]{:S(2)}) copy-start(s32[80]{0:T(128)} %param.7) | copy-start | bytes 964
  28.6 32.0 %all-to-all-start = ((f32[5,32,974]{2,0,1:T(8,128)}), f32[5,32,974]{2,0,1:T(8,128)S(1)}, u32[]{:S(2)}, u32[]{:S(2)}) async-start(f32[5,32,974]{2,0,1:T(8,128)} %copy.32), calls=%async_computation.1 | async-start | bytes 2097152 | tf_op jit(solution)/shard_map/all_to_all | solution.py:37
Sparse Core Ops, SparseCore 0:
  13.8 11.4 reduce-scatter.1
where the time goes:
time: 91.8 us; the launch traced here: 91.5 us
  waiting for transfers between devices  35.3 us (38%)
  local copies, waits for them, and re-layouts  20.2 us (22%)
  between operations  13.5 us (15%)
  matrix products  9.76 us (11%)
  starting transfers between devices  5.8 us (6%)
  blocking collectives  4.22 us (5%)
  other arithmetic  2.7 us (3%)
    all_to_all x1, waiting for transfers between devices, shards(): lax.all_to_all(mo_pairs, 'pair', split_axis=1, concat_axis=0, tiled=True)  23.9 us
    reduce_scatter x1, waiting for transfers between devices, shards(): lax.psum_scatter(partial_value, 'lam', scatter_dimension=0, tiled=True)  11.3 us
    unnamed x9, local copies, waits for them, and re-layouts  7.69 us
    dot_general x1, matrix products, shards(): jnp.einsum('li,pls->pis', occ_rows, integrals, preferred_element_type=jnp...  7.12 us
    all_to_all x1, starting transfers between devices, shards(): lax.all_to_all(mo_pairs, 'pair', split_axis=1, concat_axis=0, tiled=True)  5.79 us
    all_to_all x1, blocking collectives, shards(): lax.all_to_all(lax.all_to_all(mo_pairs, 'pair', split_axis=1, concat_axis...  4.22 us
    all_to_all x2, local copies, waits for them, and re-layouts, shards(): lax.all_to_all(mo_pairs, 'pair', split_axis=1, concat_axis=0, tiled=True)  3.92 us
    all_to_all x1, other arithmetic, shards(): lax.all_to_all(lax.all_to_all(mo_pairs, 'pair', split_axis=1, concat_axis...  2.62 us
  transfers between devices with their start and end apart: 2, of which 2 were waited for; matrix products, arithmetic and copies ran while one was open for 3% of the time, Pallas kernels for 0%

commit v1 on v0

v1 whole, which is shorter than its diff:
```python
import functools

import jax
import jax.numpy as jnp
from jax import lax
from jax.experimental import pallas as pl
from jax.experimental.pallas import tpu as pltpu
from jax.sharding import PartitionSpec as P

MUS = 2
ROWS = 16
MESH = pl.DeviceIdType.MESH
F32 = jnp.float32
BF16 = jnp.bfloat16


def iota(shape, dim):
    return lax.broadcasted_iota(jnp.int32, shape, dim)


def selector(mask):
    return jnp.where(mask, 1.0, 0.0).astype(BF16)


def dot(a, b):
    return jnp.dot(a, b, preferred_element_type=F32)


def dot_nt(a, b):
    return lax.dot_general(a, b, (((1,), (1,)), ((), ())), preferred_element_type=F32)


def kernel(
    npair, occ, per, batches,
    integrals, occ_hbm, virt_hbm, nu_ref, out_ref,
    ints, occ_ref, virt, occ_sel, weights, own, send_a, recv_a, half_rows, mo, send_b, recv_b,
    load_sem, small_sem, send_a_sem, recv_a_sem, send_b_sem, recv_b_sem,
):
    me = lax.axis_index("pair")
    core = lax.axis_index("lam")
    half = npair // 2
    local, lam_rows, nsig = ints.shape
    own_i = occ // 2
    vcols = virt.shape[1]
    acols = vcols // 2
    wide = recv_b.shape[2]
    in_batch = ROWS // per
    feeder = me // half
    is_self = feeder == core

    load_occ = pltpu.make_async_copy(occ_hbm, occ_ref, small_sem.at[0])
    load_occ.start()
    loads = [
        pltpu.make_async_copy(integrals.at[p], ints.at[p], load_sem.at[p]) for p in range(local)
    ]
    load_virt = pltpu.make_async_copy(virt_hbm, virt, small_sem.at[1])
    for p in range(local):
        loads[p].start()
        if p == min(2, local - 1):
            load_virt.start()

    barrier = pltpu.get_barrier_semaphore()
    for j in range(1, npair):
        pl.semaphore_signal(
            barrier, inc=1,
            device_id={"pair": lax.rem(me + j, npair), "lam": feeder}, device_id_type=MESH,
        )
    pl.semaphore_signal(
        barrier, inc=1, device_id={"pair": me, "lam": 1 - core}, device_id_type=MESH
    )

    load_occ.wait()
    turned = selector(
        iota((occ, occ), 1) == ((iota((occ, occ), 0) + core * own_i) & (occ - 1))
    )
    start = pl.multiple_of(core * lam_rows, lam_rows)
    occ_sel[...] = dot_nt(turned, occ_ref[pl.ds(start, lam_rows), :]).astype(BF16)

    eye = selector(iota((occ, occ), 0) == iota((occ, occ), 1))
    occ_t = dot_nt(eye, occ_ref[...]).astype(BF16)
    pairs_all = nu_ref.shape[1]
    nbasis = occ_ref.shape[0]
    picked = selector(iota((nbasis, pairs_all), 0) == nu_ref[...])
    rows_t = dot(occ_t, picked).astype(BF16)
    mrows = MUS * occ * per
    cols = npair * ROWS
    spread = selector(
        ((iota((mrows, occ), 0) // per) & (occ - 1)) == iota((mrows, occ), 1)
    )
    tall = dot(spread, rows_t).astype(BF16)
    r = iota((mrows, cols), 0)
    c = iota((mrows, cols), 1)
    width = pairs_all // MUS
    for b in range(batches):
        cp = iota((pairs_all, cols), 1)
        place = b * in_batch + (cp & (ROWS - 1)) // per
        hit = (iota((pairs_all, cols), 0) == (cp // ROWS) * local + place) & (place < local)
        full = dot(tall, selector(hit))
        pair_of = (c // ROWS) * local + b * in_batch + (c & (ROWS - 1)) // per
        keep = ((r & (per - 1)) == (c & (per - 1))) & (
            (r >= occ * per) == (pair_of >= width)
        )
        weights[b] = jnp.where(keep, full, 0.0).astype(BF16)

    tail = local - (batches - 1) * in_batch
    if tail < in_batch:
        half_rows[batches - 1] = jnp.zeros(half_rows.shape[1:], F32)
    mo[:, vcols - vcols % 128:] = jnp.zeros((mo.shape[0], mo.shape[1] - (vcols - vcols % 128)), F32)

    pl.semaphore_wait(barrier, jnp.where(is_self, 2 * half - 1, 2 * half + 1))

    def to_sibling(p):
        return pltpu.make_async_remote_copy(
            src_ref=send_a.at[p], dst_ref=recv_a.at[p],
            send_sem=send_a_sem.at[p], recv_sem=recv_a_sem.at[p],
            device_id={"pair": me, "lam": 1 - core}, device_id_type=MESH,
        )

    def first(p):
        loads[p].wait()
        value = dot(occ_sel[...], ints[p])
        send_a[p] = value[own_i:]
        to_sibling(p).start()
        own[p] = value[:own_i]

    def to_owner(b, side, j):
        k = lax.rem(me + 1 + j, half)
        return k, pltpu.make_async_remote_copy(
            src_ref=send_b.at[b, side, pl.ds(pl.multiple_of(k * ROWS, ROWS), ROWS)],
            dst_ref=recv_b.at[b, pl.ds(pl.multiple_of(me * ROWS, ROWS), ROWS)],
            send_sem=send_b_sem.at[b, side, j], recv_sem=recv_b_sem.at[b, me],
            device_id={"pair": core * half + k, "lam": side}, device_id_type=MESH,
        )

    def second(b):
        for q in range(min(in_batch, local - b * in_batch)):
            p = b * in_batch + q
            to_sibling(p).wait_recv()
            value = own[p] + recv_a[p]
            for k in range(half):
                half_rows[b, k * ROWS + q * per:k * ROWS + (q + 1) * per, :] = (
                    value[k * per:(k + 1) * per]
                )
        if b == 0:
            load_virt.wait()
        mo[:, :vcols] = dot(half_rows[b].astype(BF16), virt[...])
        base = acols // 128 * 128
        span = min(mo.shape[1] - base, wide + 128)
        upper = mo[:, base:base + span]
        upper = pltpu.roll(upper, span - (acols - base), 1)[:, :wide]
        send_b[b, 0] = mo[:, :wide].astype(BF16)
        send_b[b, 1] = upper.astype(BF16)
        for j in range(half):
            for side in range(2):
                k, copy = to_owner(b, side, j)
                if j < half - 1:
                    copy.start()
                else:
                    mine = is_self & (core == side)

                    @pl.when(jnp.logical_not(mine))
                    def _():
                        copy.start()

                    @pl.when(mine)
                    def _():
                        rows = pl.ds(pl.multiple_of(k * ROWS, ROWS), ROWS)
                        recv_b[b, pl.ds(pl.multiple_of(me * ROWS, ROWS), ROWS), :] = (
                            send_b[b, side, rows, :]
                        )

    done = 0
    for b in range(batches):
        ready = min((b + 1) * in_batch + 1, local)
        for p in range(done, ready):
            first(p)
        done = ready
        second(b)

    for b in range(batches):
        for s in range(npair):
            landed = pltpu.make_async_remote_copy(
                src_ref=recv_b.at[b, pl.ds(s * ROWS, ROWS)],
                dst_ref=recv_b.at[b, pl.ds(s * ROWS, ROWS)],
                send_sem=send_b_sem.at[b, 0, 0], recv_sem=recv_b_sem.at[b, s],
                device_id={"pair": me, "lam": 1 - core}, device_id_type=MESH,
            )

            @pl.when(jnp.logical_not(is_self & (me == s)))
            def _():
                landed.wait_recv()
        value = dot(weights[b], recv_b[b])[:, :acols]
        if b == 0:
            out_ref[...] = value
        else:
            out_ref[...] += value

    for p in range(local):
        to_sibling(p).wait_send()
    for b in range(batches):
        for j in range(half):
            for side in range(2):
                k, copy = to_owner(b, side, j)
                if j < half - 1:
                    copy.wait_send()
                else:

                    @pl.when(jnp.logical_not(is_self & (core == side)))
                    def _():
                        copy.wait_send()


def shards(npair, integrals, occ_coef, virt_coef, pair_nu):
    local, lam_rows, nsig = integrals.shape
    nbasis, occ = occ_coef.shape
    vcols = virt_coef.shape[1]
    half = npair // 2
    per = occ // npair
    in_batch = ROWS // per
    batches = -(-local // in_batch)
    acols = vcols // 2
    wide = -(-acols // 128) * 128
    vwide = -(-vcols // 128) * 128
    own_i = occ // 2
    mrows = MUS * occ * per
    anyspace = pl.BlockSpec(memory_space=pl.ANY)
    vmem = pl.BlockSpec(memory_space=pltpu.VMEM)
    out = pl.pallas_call(
        functools.partial(kernel, npair, occ, per, batches),
        out_shape=jax.ShapeDtypeStruct((mrows, acols), F32),
        in_specs=[anyspace, anyspace, anyspace, vmem],
        out_specs=vmem,
        scratch_shapes=[
            pltpu.VMEM((local, lam_rows, nsig), BF16),
            pltpu.VMEM((nbasis, occ), BF16),
            pltpu.VMEM((nsig, vcols), BF16),
            pltpu.VMEM((occ, lam_rows), BF16),
            pltpu.VMEM((batches, mrows, npair * ROWS), BF16),
            pltpu.VMEM((local, own_i, nsig), F32),
            pltpu.VMEM((local, own_i, nsig), F32),
            pltpu.VMEM((local, own_i, nsig), F32),
            pltpu.VMEM((batches, half * ROWS, nsig), F32),
            pltpu.VMEM((half * ROWS, vwide), F32),
            pltpu.VMEM((batches, 2, half * ROWS, wide), BF16),
            pltpu.VMEM((batches, npair * ROWS, wide), BF16),
            pltpu.SemaphoreType.DMA((local,)),
            pltpu.SemaphoreType.DMA((2,)),
            pltpu.SemaphoreType.DMA((local,)),
            pltpu.SemaphoreType.DMA((local,)),
            pltpu.SemaphoreType.DMA((batches, 2, half)),
            pltpu.SemaphoreType.DMA((batches, npair)),
        ],
        compiler_params=pltpu.CompilerParams(
            collective_id=0, has_side_effects=True, vmem_limit_bytes=48 * 1024 * 1024
        ),
        name="mp2_transform",
    )(integrals, occ_coef, virt_coef, pair_nu.reshape(1, -1))
    return out.reshape(MUS, occ, per, acols)


def solution(mesh):
    in_specs = (P(("groups", "pair"), "lam", None), P(), P(), P("groups"))
    out_specs = P("groups", None, "pair", "lam")
    body = functools.partial(shards, mesh.shape["pair"])
    return jax.shard_map(body, mesh=mesh, in_specs=in_specs, out_specs=out_specs, check_vma=False)
```

time: 91.8 us -> 25.3 us (0.28)
  waiting for transfers between devices: 35.3 us -> 0 us
  Pallas kernels: 0 us -> 20.2 us
  local copies, waits for them, and re-layouts: 20.2 us -> 4.82 us
  between operations: 13.5 us -> 0.04 us
  matrix products: 9.76 us -> 0 us
  starting transfers between devices: 5.8 us -> 0 us
  blocking collectives: 4.22 us -> 0 us
  other arithmetic: 2.7 us -> 0 us
    all_to_all x1 -> x0, waiting for transfers between devices: 23.9 us -> none  [shards(): lax.all_to_all(mo_pairs, 'pair', split_axis=1, concat_axis=0, tiled=True)]
    pallas_call x0 -> x1, Pallas kernels: none -> 20.2 us  [shards(): pl.pallas_call(functools.partial(kernel, npair, occ, per, batches), out_s...]
    reduce_scatter x1 -> x0, waiting for transfers between devices: 11.3 us -> none  [shards(): lax.psum_scatter(partial_value, 'lam', scatter_dimension=0, tiled=True)]
    dot_general x3 -> x0, matrix products: 9.76 us -> none  [the longest x1 7.12 us: shards(): jnp.einsum('li,pls->pis', occ_rows, integrals, preferred_element_type=jnp...]
    all_to_all x4 -> x0, local copies, waits for them, and re-layouts: 6.34 us -> none  [the longest x2 3.92 us: shards(): lax.all_to_all(mo_pairs, 'pair', split_axis=1, concat_axis=0, tiled=True)]
    all_to_all x1 -> x0, starting transfers between devices: 5.79 us -> none  [shards(): lax.all_to_all(mo_pairs, 'pair', split_axis=1, concat_axis=0, tiled=True)]
    all_to_all x1 -> x0, blocking collectives: 4.22 us -> none  [shards(): lax.all_to_all(lax.all_to_all(mo_pairs, 'pair', split_axis=1, concat_axis...]
    unnamed x9 -> x4, local copies, waits for them, and re-layouts: 7.69 us -> 3.85 us
  transfers between devices with their start and end apart: 2 -> 0, of which waited for: 2 -> 0; matrix products, arithmetic and copies ran while one was open for 3% -> 0% of each run, Pallas kernels for 0% -> 0%
where the time goes in v1:
time: 25.3 us; the launch traced here: 25.1 us
  Pallas kernels  20.2 us (80%)
  local copies, waits for them, and re-layouts  4.82 us (19%)
    pallas_call x1, Pallas kernels, shards(): pl.pallas_call(functools.partial(kernel, npair, occ, per, batches), out_s...  20.2 us
    unnamed x4, local copies, waits for them, and re-layouts  3.85 us
    reshape x1, local copies, waits for them, and re-layouts, shards(): return out.reshape(MUS, occ, per, acols)  0.96 us

profile of v1, /device:TPU:0, one launch (start us, length us, event | category | flops | bytes accessed | tf_op | source)
XLA Modules:
  0.0 25.1 jit_solution(1855314743639168503)
XLA Ops:
  0.0 1.0 %copy.7.occ_hbm = bf16[1024,32]{1,0:T(8,128)(2,1)S(1)} copy(bf16[1024,32]{0,1:T(8,128)(2,1)} %param.5) | data formatting | bytes 131072 | tf_op args[1]
  1.0 0.0 copy-start
  1.0 2.8 %copy.8.virt_hbm = bf16[1024,974]{1,0:T(8,128)(2,1)S(1)} copy(bf16[1024,974]{0,1:T(8,128)(2,1)} %param.6) | data formatting | bytes 3989504 | tf_op args[2]
  3.9 0.0 copy-done
  3.9 20.2 %mp2_transform.1 = f32[256,487]{1,0:T(8,128)S(1)} custom-call(bf16[10,512,1024]{2,1,0:T(8,128)(2,1)} %integrals.1, bf16[1024,32]{1,0:T(8,128)(2,1)S(1)} %copy.7.occ_hbm, bf16[1024,974]{1,0:T(8,128)(2,1)S(1)} %copy.8.virt_hbm, s32[1,80]{1,0:T(1,128)S(1)} %bitcast.1), custom_call_target="tpu_custom_call" | custom-call | tf_op jit(solution)/shard_map/mp2_transform/pallas_call | solution.py:228
  24.1 1.0 %reshape.7 = f32[2,32,4,487]{3,2,1,0:T(4,128)} reshape(f32[256,487]{1,0:T(8,128)S(1)} %mp2_transform.1) | data formatting | bytes 997376 | tf_op jit(solution)/shard_map/reshape | solution.py:258
Async XLA Ops:
  1.0 2.9 %copy-start = (s32[80]{0:T(128)S(1)}, s32[80]{0:T(128)}, u32[]{:S(2)}) copy-start(s32[80]{0:T(128)} %param.7) | copy-start | bytes 964

commit v2 on v1

v2 whole, which is shorter than its diff:
```python
import functools

import jax
import jax.numpy as jnp
from jax import lax
from jax.experimental import pallas as pl
from jax.experimental.pallas import tpu as pltpu
from jax.sharding import PartitionSpec as P

MUS = 2
ROWS = 16
AHEAD = 2
WINDOW = 4
VIRT_AT = 0
MESH = pl.DeviceIdType.MESH
F32 = jnp.float32
BF16 = jnp.bfloat16


def iota(shape, dim):
    return lax.broadcasted_iota(jnp.int32, shape, dim)


def selector(mask):
    return jnp.where(mask, 1.0, 0.0).astype(BF16)


def dot(a, b):
    return jnp.dot(a, b, preferred_element_type=F32)


def dot_nt(a, b):
    return lax.dot_general(a, b, (((1,), (1,)), ((), ())), preferred_element_type=F32)


def kernel(
    npair, occ, per, batches,
    integrals, occ_hbm, virt_hbm, nu_hbm, out_ref,
    ints, occ_ref, virt, nu_ref, occ_sel, weights, own, send_a, recv_a, half_rows, mo, send_b, recv_b, send_t, recv_t,
    load_sem, small_sem, send_a_sem, recv_a_sem, send_b_sem, recv_b_sem,
):
    me = lax.axis_index("pair")
    core = lax.axis_index("lam")
    half = npair // 2
    local, lam_rows, nsig = ints.shape
    own_i = occ // 2
    vcols = virt.shape[0]
    acols = vcols // 2
    wide = recv_b.shape[2]
    in_batch = ROWS // per
    feeder = me // half
    is_self = feeder == core
    tail = local - (batches - 1) * in_batch
    fold = 2 if tail * per <= ROWS // 2 else 1
    last = batches - 1
    thin = wide // 2

    def rows_of(b):
        return ROWS // fold if b == last else ROWS

    def outgoing(b):
        return send_t if b == last and fold == 2 else send_b.at[b]

    def incoming(b):
        return recv_t if b == last and fold == 2 else recv_b.at[b]

    load_occ = pltpu.make_async_copy(occ_hbm, occ_ref, small_sem.at[0])
    load_occ.start()
    loads = [
        pltpu.make_async_copy(integrals.at[p], ints.at[p], load_sem.at[p]) for p in range(local)
    ]
    load_virt = pltpu.make_async_copy(virt_hbm, virt, small_sem.at[1])
    load_nu = pltpu.make_async_copy(nu_hbm, nu_ref, small_sem.at[2])
    for p in range(min(WINDOW, local)):
        loads[p].start()

    barrier = pltpu.get_barrier_semaphore()
    for j in range(1, npair):
        pl.semaphore_signal(
            barrier, inc=1,
            device_id={"pair": lax.rem(me + j, npair), "lam": feeder}, device_id_type=MESH,
        )
    pl.semaphore_signal(
        barrier, inc=1, device_id={"pair": me, "lam": 1 - core}, device_id_type=MESH
    )

    load_occ.wait()
    turned = selector(
        iota((occ, occ), 1) == ((iota((occ, occ), 0) + core * own_i) & (occ - 1))
    )
    start = pl.multiple_of(core * lam_rows, lam_rows)
    occ_sel[...] = dot(turned, occ_ref[:, pl.ds(start, lam_rows)]).astype(BF16)

    if tail * per < rows_of(last):
        half_rows[last] = jnp.zeros(half_rows.shape[1:], F32)
    mo[:, vcols - vcols % 128:] = jnp.zeros((mo.shape[0], mo.shape[1] - (vcols - vcols % 128)), F32)

    pl.semaphore_wait(barrier, jnp.where(is_self, 2 * half - 1, 2 * half + 1))

    def to_sibling(p):
        return pltpu.make_async_remote_copy(
            src_ref=send_a.at[p], dst_ref=recv_a.at[p],
            send_sem=send_a_sem.at[p], recv_sem=recv_a_sem.at[p],
            device_id={"pair": me, "lam": 1 - core}, device_id_type=MESH,
        )

    def first(p):
        loads[p].wait()
        if p + WINDOW < local:
            loads[p + WINDOW].start()
        if p == VIRT_AT:
            load_virt.start()
            load_nu.start()
        value = dot(occ_sel[...], ints[p])
        send_a[p] = value[own_i:]
        to_sibling(p).start()
        own[p] = value[:own_i]

    def to_owner(b, side, j):
        k = lax.rem(me + 1 + j, half)
        return k, pltpu.make_async_remote_copy(
            src_ref=outgoing(b).at[side, pl.ds(pl.multiple_of(k * ROWS, ROWS), ROWS)],
            dst_ref=incoming(b).at[pl.ds(pl.multiple_of(me * ROWS, ROWS), ROWS)],
            send_sem=send_b_sem.at[b, side, j], recv_sem=recv_b_sem.at[b, me],
            device_id={"pair": core * half + k, "lam": side}, device_id_type=MESH,
        )

    def second(b):
        size = rows_of(b)
        count = half * size
        for q in range(min(in_batch, local - b * in_batch)):
            p = b * in_batch + q
            to_sibling(p).wait_recv()
            value = own[p] + recv_a[p]
            for k in range(half):
                half_rows[b, k * size + q * per:k * size + (q + 1) * per, :] = (
                    value[k * per:(k + 1) * per]
                )
        if b == 0:
            load_virt.wait()
        mo[:count, :vcols] = dot_nt(half_rows[b, :count].astype(BF16), virt[...])
        base = acols // 128 * 128
        span = min(mo.shape[1] - base, wide + 128)
        upper = mo[:count, base:base + span]
        upper = pltpu.roll(upper, span - (acols - base), 1)[:, :wide]
        for side, value in enumerate((mo[:count, :wide], upper)):
            if size < ROWS:
                value = jnp.concatenate(
                    [
                        value[k * size:(k + 1) * size, h * thin:(h + 1) * thin]
                        for k in range(half) for h in range(2)
                    ],
                    axis=0,
                )
            outgoing(b)[side] = value.astype(BF16)
        for j in range(half):
            for side in range(2):
                k, copy = to_owner(b, side, j)
                if j < half - 1:
                    copy.start()
                else:
                    mine = is_self & (core == side)

                    @pl.when(jnp.logical_not(mine))
                    def _():
                        copy.start()

                    @pl.when(mine)
                    def _():
                        rows = pl.ds(pl.multiple_of(k * ROWS, ROWS), ROWS)
                        incoming(b)[pl.ds(pl.multiple_of(me * ROWS, ROWS), ROWS), :] = (
                            outgoing(b)[side, rows, :]
                        )

    done = 0
    for b in range(batches):
        ready = min((b + 1) * in_batch + AHEAD, local)
        for p in range(done, ready):
            first(p)
        done = ready
        second(b)

    load_nu.wait()
    pairs_all = nu_ref.shape[1]
    nbasis = occ_ref.shape[1]
    picked = selector(iota((nbasis, pairs_all), 0) == nu_ref[...])
    rows_t = dot(occ_ref[...], picked).astype(BF16)
    mrows = MUS * occ * per
    cols = npair * ROWS
    spread = selector(
        ((iota((mrows, occ), 0) // per) & (occ - 1)) == iota((mrows, occ), 1)
    )
    tall = dot(spread, rows_t).astype(BF16)
    r = iota((mrows, cols), 0)
    c = iota((mrows, cols), 1)
    width = pairs_all // MUS
    for n in range(batches + fold - 1):
        b = min(n, last)
        size = rows_of(b)
        cp = iota((pairs_all, cols), 1)
        place = b * in_batch + (cp & (size - 1)) // per
        hit = (iota((pairs_all, cols), 0) == (cp // ROWS) * local + place) & (place < local)
        if size < ROWS:
            hit = hit & ((cp & (ROWS - 1)) // size == n - b)
        full = dot(tall, selector(hit))
        pair_of = (c // ROWS) * local + b * in_batch + (c & (size - 1)) // per
        keep = ((r & (per - 1)) == (c & (per - 1))) & (
            (r >= occ * per) == (pair_of >= width)
        )
        weights[n] = jnp.where(keep, full, 0.0).astype(BF16)

    for b in range(batches):
        for s in range(npair):
            landed = pltpu.make_async_remote_copy(
                src_ref=incoming(b).at[pl.ds(s * ROWS, ROWS)],
                dst_ref=incoming(b).at[pl.ds(s * ROWS, ROWS)],
                send_sem=send_b_sem.at[b, 0, 0], recv_sem=recv_b_sem.at[b, s],
                device_id={"pair": me, "lam": 1 - core}, device_id_type=MESH,
            )

            @pl.when(jnp.logical_not(is_self & (me == s)))
            def _():
                landed.wait_recv()
        if rows_of(b) < ROWS:
            value = jnp.concatenate([dot(weights[b + h], recv_t[...]) for h in range(2)], axis=1)
        else:
            value = dot(weights[b], recv_b[b])
        if b == 0:
            out_ref[...] = value[:, :acols]
        else:
            out_ref[...] += value[:, :acols]

    for p in range(local):
        to_sibling(p).wait_send()
    for b in range(batches):
        for j in range(half):
            for side in range(2):
                k, copy = to_owner(b, side, j)
                if j < half - 1:
                    copy.wait_send()
                else:

                    @pl.when(jnp.logical_not(is_self & (core == side)))
                    def _():
                        copy.wait_send()


def shards(npair, integrals, occ_coef, virt_coef, pair_nu):
    local, lam_rows, nsig = integrals.shape
    nbasis = occ_coef.shape[0]
    occ = occ_coef.shape[1]
    vcols = virt_coef.shape[1]
    half = npair // 2
    per = occ // npair
    in_batch = ROWS // per
    batches = -(-local // in_batch)
    acols = vcols // 2
    wide = -(-acols // 128) * 128
    vwide = -(-vcols // 128) * 128
    own_i = occ // 2
    mrows = MUS * occ * per
    pairs_all = pair_nu.shape[0]
    hbm = pl.BlockSpec(memory_space=pltpu.HBM)
    vmem = pl.BlockSpec(memory_space=pltpu.VMEM)
    out = pl.pallas_call(
        functools.partial(kernel, npair, occ, per, batches),
        out_shape=jax.ShapeDtypeStruct((mrows, acols), F32),
        in_specs=[hbm, hbm, hbm, hbm],
        out_specs=vmem,
        scratch_shapes=[
            pltpu.VMEM((local, lam_rows, nsig), BF16),
            pltpu.VMEM((occ, nbasis), BF16),
            pltpu.VMEM((vcols, nsig), BF16),
            pltpu.VMEM((1, pairs_all), jnp.int32),
            pltpu.VMEM((occ, lam_rows), BF16),
            pltpu.VMEM((batches + 1, mrows, npair * ROWS), BF16),
            pltpu.VMEM((local, own_i, nsig), F32),
            pltpu.VMEM((local, own_i, nsig), F32),
            pltpu.VMEM((local, own_i, nsig), F32),
            pltpu.VMEM((batches, half * ROWS, nsig), F32),
            pltpu.VMEM((half * ROWS, vwide), F32),
            pltpu.VMEM((batches, 2, half * ROWS, wide), BF16),
            pltpu.VMEM((batches, npair * ROWS, wide), BF16),
            pltpu.VMEM((2, half * ROWS, wide // 2), BF16),
            pltpu.VMEM((npair * ROWS, wide // 2), BF16),
            pltpu.SemaphoreType.DMA((local,)),
            pltpu.SemaphoreType.DMA((3,)),
            pltpu.SemaphoreType.DMA((local,)),
            pltpu.SemaphoreType.DMA((local,)),
            pltpu.SemaphoreType.DMA((batches, 2, half)),
            pltpu.SemaphoreType.DMA((batches, npair)),
        ],
        compiler_params=pltpu.CompilerParams(
            collective_id=0, has_side_effects=True, vmem_limit_bytes=64 * 1024 * 1024
        ),
        name="mp2_transform",
    )(integrals, occ_coef.T, virt_coef.T, pair_nu.reshape(1, -1))
    return out.reshape(MUS, occ, per, acols)


def solution(mesh):
    in_specs = (P(("groups", "pair"), "lam", None), P(), P(), P("groups"))
    out_specs = P("groups", None, "pair", "lam")
    body = functools.partial(shards, mesh.shape["pair"])
    return jax.shard_map(body, mesh=mesh, in_specs=in_specs, out_specs=out_specs, check_vma=False)
```

time: 25.3 us -> 22.5 us (0.89)
  local copies, waits for them, and re-layouts: 4.82 us -> 2 us
    unnamed x4 -> x0, local copies, waits for them, and re-layouts: 3.85 us -> none
    reshape x1, local copies, waits for them, and re-layouts: 0.96 us -> 2 us  [shards(): return out.reshape(MUS, occ, per, acols)]
where the time goes in v2:
time: 22.5 us; the launch traced here: 22.4 us
  Pallas kernels  20.4 us (91%)
  local copies, waits for them, and re-layouts  2 us (9%)
    pallas_call x1, Pallas kernels, shards(): pl.pallas_call(functools.partial(kernel, npair, occ, per, batches), out_s...  20.4 us
    reshape x1, local copies, waits for them, and re-layouts, shards(): return out.reshape(MUS, occ, per, acols)  2 us

profile of v2, /device:TPU:0, one launch (start us, length us, event | category | flops | bytes accessed | tf_op | source)
XLA Modules:
  0.0 22.4 jit_solution(16036095052918463679)
XLA Ops:
  0.0 20.4 %mp2_transform.1 = f32[256,487]{1,0:T(8,128)} custom-call(bf16[10,512,1024]{2,1,0:T(8,128)(2,1)} %integrals.1, bf16[32,1024]{1,0:T(8,128)(2,1)} %bitcast.4, bf16[974,1024]{1,0:T(8,128)(2,1)} %bitcast.3, s32[1,80]{1,0:T(1,128)} %bitcast.5), custom_call_target="tpu_custom_call" | custom-call | tf_op jit(solution)/shard_map/mp2_transform/pallas_call | solution.py:265
  20.4 2.0 %reshape.7 = f32[2,32,4,487]{3,2,1,0:T(4,128)} reshape(f32[256,487]{1,0:T(8,128)} %mp2_transform.1) | data formatting | bytes 997376 | tf_op jit(solution)/shard_map/reshape | solution.py:298

commit v3 on v2

--- a/solution.py
+++ b/solution.py
@@ -9,9 +9,10 @@
 
 MUS = 2
 ROWS = 16
-AHEAD = 2
-WINDOW = 4
-VIRT_AT = 0
+AHEAD = 0
+LIMIT = 64 * 1024 * 1024
+WINDOW = 5
+VIRT_AT = 1
 MESH = pl.DeviceIdType.MESH
 F32 = jnp.float32
 BF16 = jnp.bfloat16
@@ -35,9 +36,9 @@
 
 def kernel(
     npair, occ, per, batches,
-    integrals, occ_hbm, virt_hbm, nu_hbm, out_ref,
-    ints, occ_ref, virt, nu_ref, occ_sel, weights, own, send_a, recv_a, half_rows, mo, send_b, recv_b, send_t, recv_t,
-    load_sem, small_sem, send_a_sem, recv_a_sem, send_b_sem, recv_b_sem,
+    integrals, occ_hbm, virt_hbm, nu_hbm, recv_b, recv_t, weights_out,
+    ints, occ_ref, virt, nu_ref, occ_sel, weights, own, send_a, recv_a, half_rows, mo, send_b, send_t,
+    load_sem, small_sem, send_a_sem, recv_a_sem, send_b_sem, recv_b_sem, own_sem,
 ):
     me = lax.axis_index("pair")
     core = lax.axis_index("lam")
@@ -46,7 +47,7 @@
     own_i = occ // 2
     vcols = virt.shape[0]
     acols = vcols // 2
-    wide = recv_b.shape[2]
+    wide = send_b.shape[3]
     in_batch = ROWS // per
     feeder = me // half
     is_self = feeder == core
@@ -123,6 +124,13 @@
             dst_ref=incoming(b).at[pl.ds(pl.multiple_of(me * ROWS, ROWS), ROWS)],
             send_sem=send_b_sem.at[b, side, j], recv_sem=recv_b_sem.at[b, me],
             device_id={"pair": core * half + k, "lam": side}, device_id_type=MESH,
+        )
+
+    def keep_own(b, side, k):
+        return pltpu.make_async_copy(
+            outgoing(b).at[side, pl.ds(pl.multiple_of(k * ROWS, ROWS), ROWS)],
+            incoming(b).at[pl.ds(pl.multiple_of(me * ROWS, ROWS), ROWS)],
+            own_sem.at[b, side],
         )
 
     def second(b):
@@ -167,10 +175,7 @@
 
                     @pl.when(mine)
                     def _():
-                        rows = pl.ds(pl.multiple_of(k * ROWS, ROWS), ROWS)
-                        incoming(b)[pl.ds(pl.multiple_of(me * ROWS, ROWS), ROWS), :] = (
-                            outgoing(b)[side, rows, :]
-                        )
+                        keep_own(b, side, k).start()
 
     done = 0
     for b in range(batches):
@@ -209,6 +214,8 @@
         )
         weights[n] = jnp.where(keep, full, 0.0).astype(BF16)
 
+    save = pltpu.make_async_copy(weights, weights_out, small_sem.at[0])
+    save.start()
     for b in range(batches):
         for s in range(npair):
             landed = pltpu.make_async_remote_copy(
@@ -221,15 +228,7 @@
             @pl.when(jnp.logical_not(is_self & (me == s)))
             def _():
                 landed.wait_recv()
-        if rows_of(b) < ROWS:
-            value = jnp.concatenate([dot(weights[b + h], recv_t[...]) for h in range(2)], axis=1)
-        else:
-            value = dot(weights[b], recv_b[b])
-        if b == 0:
-            out_ref[...] = value[:, :acols]
-        else:
-            out_ref[...] += value[:, :acols]
-
+    save.wait()
     for p in range(local):
         to_sibling(p).wait_send()
     for b in range(batches):
@@ -240,9 +239,29 @@
                     copy.wait_send()
                 else:
 
-                    @pl.when(jnp.logical_not(is_self & (core == side)))
+                    mine = is_self & (core == side)
+
+                    @pl.when(jnp.logical_not(mine))
                     def _():
                         copy.wait_send()
+
+                    @pl.when(mine)
+                    def _():
+                        keep_own(b, side, k).wait()
+
+
+def finish(recv_b, recv_t, weights, out_ref):
+    batches = recv_b.shape[0]
+    acols = out_ref.shape[-1]
+    total = None
+    full = batches - (weights.shape[0] - batches)
+    for b in range(full):
+        value = dot(weights[b], recv_b[b])
+        total = value if total is None else total + value
+    if full < batches:
+        value = jnp.concatenate([dot(weights[full + h], recv_t[...]) for h in range(2)], axis=1)
+        total = value if total is None else total + value
+    out_ref[...] = total[:, :acols].reshape(out_ref.shape)
 
 
 def shards(npair, integrals, occ_coef, virt_coef, pair_nu):
@@ -260,42 +279,55 @@
     own_i = occ // 2
     mrows = MUS * occ * per
     pairs_all = pair_nu.shape[0]
+    tail = local - (batches - 1) * in_batch
+    terms = batches + (1 if tail * per <= ROWS // 2 else 0)
+    anyspace = pl.BlockSpec(memory_space=pl.ANY)
     hbm = pl.BlockSpec(memory_space=pltpu.HBM)
     vmem = pl.BlockSpec(memory_space=pltpu.VMEM)
-    out = pl.pallas_call(
+    recv_b, recv_t, weights = pl.pallas_call(
         functools.partial(kernel, npair, occ, per, batches),
-        out_shape=jax.ShapeDtypeStruct((mrows, acols), F32),
+        out_shape=(
+            jax.ShapeDtypeStruct((batches, npair * ROWS, wide), BF16),
+            jax.ShapeDtypeStruct((npair * ROWS, wide // 2), BF16),
+            jax.ShapeDtypeStruct((terms, mrows, npair * ROWS), BF16),
+        ),
         in_specs=[hbm, hbm, hbm, hbm],
-        out_specs=vmem,
+        out_specs=(anyspace, anyspace, anyspace),
         scratch_shapes=[
             pltpu.VMEM((local, lam_rows, nsig), BF16),
             pltpu.VMEM((occ, nbasis), BF16),
             pltpu.VMEM((vcols, nsig), BF16),
             pltpu.VMEM((1, pairs_all), jnp.int32),
             pltpu.VMEM((occ, lam_rows), BF16),
-            pltpu.VMEM((batches + 1, mrows, npair * ROWS), BF16),
+            pltpu.VMEM((terms, mrows, npair * ROWS), BF16),
             pltpu.VMEM((local, own_i, nsig), F32),
             pltpu.VMEM((local, own_i, nsig), F32),
             pltpu.VMEM((local, own_i, nsig), F32),
             pltpu.VMEM((batches, half * ROWS, nsig), F32),
             pltpu.VMEM((half * ROWS, vwide), F32),
             pltpu.VMEM((batches, 2, half * ROWS, wide), BF16),
-            pltpu.VMEM((batches, npair * ROWS, wide), BF16),
             pltpu.VMEM((2, half * ROWS, wide // 2), BF16),
-            pltpu.VMEM((npair * ROWS, wide // 2), BF16),
             pltpu.SemaphoreType.DMA((local,)),
             pltpu.SemaphoreType.DMA((3,)),
             pltpu.SemaphoreType.DMA((local,)),
             pltpu.SemaphoreType.DMA((local,)),
             pltpu.SemaphoreType.DMA((batches, 2, half)),
             pltpu.SemaphoreType.DMA((batches, npair)),
+            pltpu.SemaphoreType.DMA((batches, 2)),
         ],
         compiler_params=pltpu.CompilerParams(
-            collective_id=0, has_side_effects=True, vmem_limit_bytes=64 * 1024 * 1024
+            collective_id=0, has_side_effects=True, vmem_limit_bytes=LIMIT
         ),
         name="mp2_transform",
     )(integrals, occ_coef.T, virt_coef.T, pair_nu.reshape(1, -1))
-    return out.reshape(MUS, occ, per, acols)
+    return pl.pallas_call(
+        finish,
+        out_shape=jax.ShapeDtypeStruct((MUS, occ, per, acols), F32),
+        in_specs=[vmem, vmem, vmem],
+        out_specs=vmem,
+        compiler_params=pltpu.CompilerParams(vmem_limit_bytes=LIMIT),
+        name="pair_contraction",
+    )(recv_b, recv_t, weights)
 
 
 def solution(mesh):

time: 22.5 us -> 21.7 us (0.964)
  local copies, waits for them, and re-layouts: 2 us -> 0 us
  Pallas kernels: 20.4 us -> 21.6 us
    pallas_call x0 -> x1, Pallas kernels: none -> 2.25 us  [shards(): pl.pallas_call(finish, out_shape=jax.ShapeDtypeStruct((MUS, occ, per, aco...]
    reshape x1 -> x0, local copies, waits for them, and re-layouts: 2 us -> none  [shards(): return out.reshape(MUS, occ, per, acols)]
    pallas_call x1, Pallas kernels: 20.4 us -> 19.3 us  [shards(): pl.pallas_call(functools.partial(kernel, npair, occ, per, batches), out_s...]
where the time goes in v3:
time: 21.7 us; the launch traced here: 21.6 us
  Pallas kernels  21.6 us (100%)
    pallas_call x1, Pallas kernels, shards(): pl.pallas_call(functools.partial(kernel, npair, occ, per, batches), out_s...  19.3 us
    pallas_call x1, Pallas kernels, shards(): pl.pallas_call(finish, out_shape=jax.ShapeDtypeStruct((MUS, occ, per, aco...  2.25 us

profile of v3, /device:TPU:0, one launch (start us, length us, event | category | flops | bytes accessed | tf_op | source)
XLA Modules:
  0.0 21.6 jit_solution(4830011796642571733)
XLA Ops:
  0.0 19.3 %mp2_transform.1 = (bf16[3,128,512]{2,1,0:T(8,128)(2,1)}, bf16[128,256]{1,0:T(8,128)(2,1)}, bf16[4,256,128]{2,1,0:T(8,128)(2,1)}) custom-call(bf16[10,512,1024]{2,1,0:T(8,128)(2,1)} %integrals.1, bf16[32,1024]{1,0:T(8,128)(2,1)} %bitcast.4, bf16[974,1024]{1,0:T(8,128)(2,1)} %bitcast.3, s32[1,80]{1,0:T(1,128)} %bitcast.5), custom_call_target="tpu_custom_call" | custom-call | tf_op jit(solution)/shard_map/mp2_transform/pallas_call | solution.py:287
  19.4 2.3 %pair_contraction.1 = f32[2,32,4,487]{3,2,1,0:T(4,128)} custom-call(bf16[3,128,512]{2,1,0:T(8,128)(2,1)} %get-tuple-element.8.recv_b, bf16[128,256]{1,0:T(8,128)(2,1)} %get-tuple-element.9.recv_t, bf16[4,256,128]{2,1,0:T(8,128)(2,1)} %get-tuple-element.10.weights), custom_call_target="tpu_custom_call" | custom-call | tf_op jit(solution)/shard_map/pair_contraction/pallas_call | solution.py:323

commit v4 on v3

--- a/solution.py
+++ b/solution.py
@@ -250,15 +250,13 @@
                         keep_own(b, side, k).wait()
 
 
-def finish(recv_b, recv_t, weights, out_ref):
-    batches = recv_b.shape[0]
+def finish(full, folded, recv_b, recv_t, weights, out_ref):
     acols = out_ref.shape[-1]
     total = None
-    full = batches - (weights.shape[0] - batches)
     for b in range(full):
         value = dot(weights[b], recv_b[b])
         total = value if total is None else total + value
-    if full < batches:
+    if folded:
         value = jnp.concatenate([dot(weights[full + h], recv_t[...]) for h in range(2)], axis=1)
         total = value if total is None else total + value
     out_ref[...] = total[:, :acols].reshape(out_ref.shape)
@@ -287,7 +285,7 @@
     recv_b, recv_t, weights = pl.pallas_call(
         functools.partial(kernel, npair, occ, per, batches),
         out_shape=(
-            jax.ShapeDtypeStruct((batches, npair * ROWS, wide), BF16),
+            jax.ShapeDtypeStruct((max(2 * batches - terms, 1), npair * ROWS, wide), BF16),
             jax.ShapeDtypeStruct((npair * ROWS, wide // 2), BF16),
             jax.ShapeDtypeStruct((terms, mrows, npair * ROWS), BF16),
         ),
@@ -321,7 +319,7 @@
         name="mp2_transform",
     )(integrals, occ_coef.T, virt_coef.T, pair_nu.reshape(1, -1))
     return pl.pallas_call(
-        finish,
+        functools.partial(finish, 2 * batches - terms, terms > batches),
         out_shape=jax.ShapeDtypeStruct((MUS, occ, per, acols), F32),
         in_specs=[vmem, vmem, vmem],
         out_specs=vmem,

time: 21.7 us -> 21.7 us (level)
  no operation moved by 1% of the time
where the time goes in v4:
time: 21.7 us; the launch traced here: 21.6 us
  Pallas kernels  21.6 us (100%)
    pallas_call x1, Pallas kernels, shards(): pl.pallas_call(functools.partial(kernel, npair, occ, per, batches), out_s...  19.3 us
    pallas_call x1, Pallas kernels, shards(): pl.pallas_call(functools.partial(finish, 2 * batches - terms, terms > bat...  2.21 us

profile of v4, /device:TPU:0, one launch (start us, length us, event | category | flops | bytes accessed | tf_op | source)
XLA Modules:
  0.0 21.6 jit_solution(2949871191997181375)
XLA Ops:
  0.0 19.3 %mp2_transform.1 = (bf16[2,128,512]{2,1,0:T(8,128)(2,1)}, bf16[128,256]{1,0:T(8,128)(2,1)}, bf16[4,256,128]{2,1,0:T(8,128)(2,1)}) custom-call(bf16[10,512,1024]{2,1,0:T(8,128)(2,1)} %integrals.1, bf16[32,1024]{1,0:T(8,128)(2,1)} %bitcast.4, bf16[974,1024]{1,0:T(8,128)(2,1)} %bitcast.3, s32[1,80]{1,0:T(1,128)} %bitcast.5), custom_call_target="tpu_custom_call" | custom-call | tf_op jit(solution)/shard_map/mp2_transform/pallas_call | solution.py:285
  19.4 2.2 %pair_contraction.1 = f32[2,32,4,487]{3,2,1,0:T(4,128)} custom-call(bf16[2,128,512]{2,1,0:T(8,128)(2,1)} %get-tuple-element.8.recv_b, bf16[128,256]{1,0:T(8,128)(2,1)} %get-tuple-element.9.recv_t, bf16[4,256,128]{2,1,0:T(8,128)(2,1)} %get-tuple-element.10.weights), custom_call_target="tpu_custom_call" | custom-call | tf_op jit(solution)/shard_map/pair_contraction/pallas_call | solution.py:321
